TPU v7x, 128 devices: a whole 4x4x4 slice. The times are simulated.
128 devices in a mesh: segment: 2 (over z_hi), dp: 16 (over x, y), mp: 4 (over z_lo, core).
Axes of the slice: x: 4, y: 4, z: 4 (z_hi: 2, z_lo: 2; z = z_hi * 2 + z_lo), core: 2. Of those that a mesh axis runs over, the one named last changes fastest.
Arguments:
- token_ids: int32 [2, 256], replicated, may hold values from 0 to 32767
- table: bfloat16 [32768, 8192], P('dp', 'mp'), may hold values from -6 to 6
- w_up: bfloat16 [2, 8192, 32768], P('segment', 'mp', 'dp'), may hold values from -0.0625 to 0.0625
- w_down: bfloat16 [2, 32768, 8192], P('segment', 'dp', 'mp'), may hold values from -0.03125 to 0.03125
- cotangent: bfloat16 [2, 256, 8192], P(None, 'dp', 'mp'), may hold values from -6 to 6
Outputs:
- acts: bfloat16 [2, 2, 256, 8192], P('segment', None, 'dp', 'mp')
- grads: bfloat16 [2, 2, 256, 8192], P('segment', None, 'dp', 'mp')
All inputs are finite; a program needn't handle non-finite values.
Results may differ from a plain program's by a relative error of at most 0.018.
Values may be sent and summed in bfloat16 or wider, within the bound.
No kernel may reach another device: no remote copies, remote signals or barrier semaphores. Data moves between devices by JAX's collectives and lax.ppermute only.
A program may use at most 128 MiB of HBM per device.

v0:
```python
import functools

import jax
import jax.numpy as jnp
from jax import lax
from jax.experimental import pallas as pl
from jax.experimental.pallas import tpu as pltpu
from jax.sharding import PartitionSpec as P

root_coef = 0.7978845608028654
bf16, f32 = jnp.bfloat16, jnp.float32
tile = 512
cost = pl.CostEstimate(flops=200_000_000, bytes_accessed=1_000_000, transcendentals=0)
params = pltpu.CompilerParams(vmem_limit_bytes=44 * 1024 * 1024)


def gelu_value(value):
    return 0.5 * value * (1.0 + jnp.tanh(root_coef * (value + 0.044715 * value * value * value)))


def gelu_slope(value):
    inner = jnp.tanh(root_coef * (value + 0.044715 * value * value * value))
    return 0.5 * (1.0 + inner) + 0.5 * value * (1.0 - inner * inner) * root_coef * (
        1.0 + 0.134145 * value * value
    )


def swap(value, bit):
    return lax.ppermute(value, "mp", [(i, i ^ bit) for i in range(4)])


def across(value):
    return lax.ppermute(value, "segment", [(0, 1), (1, 0)])


def exchange(blocks):
    return lax.all_to_all(blocks, "dp", 0, 0)


def spread(own):
    return jnp.broadcast_to(own[None], (lax.axis_size("dp"),) + own.shape)


def collect(blocks):
    return jnp.sum(blocks.astype(f32), axis=0)


def plus(own, blocks):
    return (own.astype(f32) + collect(blocks)).astype(bf16)


def multiply(rows, weight, dim):
    return lax.dot_general(
        rows, weight, (((1,), (dim,)), ((), ())), preferred_element_type=f32
    )


def start_weight(weight, dim, held, arrived):
    copies = []
    for index in range(held.shape[0]):
        columns = pl.ds(index * tile, tile)
        source = weight.at[:, columns] if dim == 0 else weight.at[columns, :]
        copies.append(pltpu.make_async_copy(source, held.at[index], arrived.at[index]))
        copies[-1].start()
    return copies


def split_tiles(rows, copies, held, dim, low, staged_kept, staged_sent, kept, sent, left):
    half = kept.shape[0]
    for index, copy in enumerate(copies):
        copy.wait()
        total = multiply(rows[...], held[index], dim)
        columns = slice(index * tile, (index + 1) * tile)
        staged_kept[:, columns] = jnp.where(low, total[:half], total[half:]).astype(bf16)
        staged_sent[:, columns] = jnp.where(low, total[half:], total[:half]).astype(bf16)
    pending = [
        pltpu.make_async_copy(staged_sent, sent, left.at[0]),
        pltpu.make_async_copy(staged_kept, kept, left.at[1]),
    ]
    for copy in pending:
        copy.start()
    for copy in pending:
        copy.wait()


def held_shape(weight, dim):
    depth, count = weight.shape[dim], weight.shape[1 - dim]
    return (count // tile, depth, tile) if dim == 0 else (count // tile, tile, depth)


def split_kernel(dim, place, rows_in, weight, kept, sent, rows, *refs):
    staged_kept, staged_sent, arrived, left, held = refs
    rows_copy = pltpu.make_async_copy(rows_in, rows, arrived.at[arrived.shape[0] - 1])
    rows_copy.start()
    copies = start_weight(weight, dim, held, arrived)
    rows_copy.wait()
    low = place[0] == 0
    split_tiles(rows, copies, held, dim, low, staged_kept, staged_sent, kept, sent, left)


def enter_kernel(place, spot, slot_in, up, down, kept, sent, own, rows, *refs):
    staged_kept, staged_sent, arrived, left, held_up, held_down, slot = refs
    slot_copy = pltpu.make_async_copy(slot_in, slot, arrived.at[arrived.shape[0] - 1])
    slot_copy.start()
    low = place[0] == 0
    tok = own.shape[0] // 2

    def run(weight, dim, held):
        copies = start_weight(weight, dim, held, arrived)
        index = lax.broadcasted_iota(jnp.int32, (rows.shape[0], slot.shape[0]), 1)
        chosen = jnp.where(index == spot[...], 1.0, 0.0).astype(bf16)
        slot_copy.wait()
        rows[...] = multiply(chosen, slot[...], 0).astype(bf16)
        quarter = rows.shape[0] // 4
        first = place[2] * tok
        first = first + jnp.where(first >= quarter, quarter, 0)
        for m in range(2):
            begin = pl.multiple_of(first + m * quarter, tok)
            own[m * tok : (m + 1) * tok] = rows[pl.ds(begin, tok)]
        split_tiles(rows, copies, held, dim, low, staged_kept, staged_sent, kept, sent, left)

    @pl.when(place[1] == 0)
    def _():
        run(up, 0, held_up)

    @pl.when(place[1] != 0)
    def _():
        run(down, 1, held_down)


anywhere = pl.BlockSpec(memory_space=pl.ANY)
scalars = pl.BlockSpec(memory_space=pltpu.SMEM)
in_vmem = pl.BlockSpec(memory_space=pltpu.VMEM)


def split_parts(count, rows, depth):
    tiles, half = count // tile, rows // 2
    out = [jax.ShapeDtypeStruct((half, count), bf16)] * 2
    scratch = [
        pltpu.VMEM((rows, depth), bf16),
        pltpu.VMEM((half, count), bf16),
        pltpu.VMEM((half, count), bf16),
        pltpu.SemaphoreType.DMA((tiles + 1,)),
        pltpu.SemaphoreType.DMA((2,)),
    ]
    return out, scratch


def split_product(rows, weight, dim, place):
    out, scratch = split_parts(weight.shape[1 - dim], *rows.shape)
    return pl.pallas_call(
        functools.partial(split_kernel, dim),
        in_specs=[scalars, anywhere, anywhere],
        out_specs=[anywhere, anywhere],
        out_shape=out,
        scratch_shapes=scratch + [pltpu.VMEM(held_shape(weight, dim), bf16)],
        compiler_params=params,
        cost_estimate=cost,
    )(place, rows, weight)


def enter_product(spot, slot, up, down, tok, place):
    out, scratch = split_parts(up.shape[1], spot.shape[0], slot.shape[1])
    return pl.pallas_call(
        enter_kernel,
        in_specs=[scalars, in_vmem, anywhere, anywhere, anywhere],
        out_specs=[anywhere, anywhere, in_vmem],
        out_shape=out + [jax.ShapeDtypeStruct((2 * tok, slot.shape[1]), bf16)],
        scratch_shapes=scratch
        + [
            pltpu.VMEM(held_shape(up, 0), bf16),
            pltpu.VMEM(held_shape(down, 1), bf16),
            pltpu.VMEM(slot.shape, bf16),
        ],
        compiler_params=params,
        cost_estimate=cost,
    )(place, spot, slot, up, down)


def rank_kernel(table_rows, place, row_ids, column_ids, spot, wanted, most):
    count, capacity = spot.shape[0], wanted.shape[0]
    shift = table_rows.bit_length() - 1
    across_ids, down_ids = row_ids[...], column_ids[...]
    here = lax.broadcasted_iota(jnp.int32, (count, count), 0)
    there = lax.broadcasted_iota(jnp.int32, (count, count), 1)
    equal = across_ids == down_ids
    same = (across_ids >> shift) == (down_ids >> shift)

    def ones(mask):
        return jnp.where(mask, 1.0, 0.0)

    repeat_down = jnp.sum(ones(equal & (there < here)), axis=1, keepdims=True)
    repeat_across = jnp.sum(ones(equal & (here < there)), axis=0, keepdims=True)
    number = jnp.sum(
        ones(same & (here < there) & (repeat_down == 0.0)), axis=0, keepdims=True
    )
    mine = jnp.sum(
        jnp.where(equal & (repeat_across == 0.0), number, 0.0), axis=1, keepdims=True
    )
    spot[...] = (down_ids >> shift) * capacity + mine.astype(jnp.int32)
    slot = lax.broadcasted_iota(jnp.int32, (capacity, count), 0)
    local = across_ids - (place[2] << shift)
    named = (
        (local >= 0)
        & (local < table_rows)
        & (repeat_across == 0.0)
        & (number.astype(jnp.int32) == slot)
    )
    wanted[...] = (
        jnp.sum(jnp.where(named, local.astype(f32) + 1.0, 0.0), axis=1, keepdims=True) - 1.0
    ).astype(jnp.int32)
    most[...] = jnp.max(mine, axis=0, keepdims=True).astype(jnp.int32) + 1


def rank(ids, table_rows, capacity, place):
    count = ids.shape[0]
    return pl.pallas_call(
        functools.partial(rank_kernel, table_rows),
        in_specs=[scalars, in_vmem, in_vmem],
        out_specs=[in_vmem] * 3,
        out_shape=[
            jax.ShapeDtypeStruct((count, 1), jnp.int32),
            jax.ShapeDtypeStruct((capacity, 1), jnp.int32),
            jax.ShapeDtypeStruct((1, 1), jnp.int32),
        ],
        compiler_params=params,
        cost_estimate=cost,
    )(place, ids[None, :], ids[:, None])


def join_kernel(dim, swapped, place, mine, other, weight, *refs):
    if swapped:
        instead, refs = refs[0], refs[1:]
    out, rows, staged, arrived, left, held = refs
    half = mine.shape[0]
    tiles = held.shape[0]

    def run():
        parts = [
            pltpu.make_async_copy(
                part,
                rows.at[pl.ds(pl.multiple_of(position * half, half), half)],
                arrived.at[tiles + index],
            )
            for index, (part, position) in enumerate(((mine, place[0]), (other, 1 - place[0])))
        ]
        for copy in parts:
            copy.start()
        copies = start_weight(weight, dim, held, arrived)
        for copy in parts:
            copy.wait()
        for index, copy in enumerate(copies):
            copy.wait()
            columns = slice(index * tile, (index + 1) * tile)
            staged[:, columns] = multiply(rows[...], held[index], dim).astype(bf16)
        done = pltpu.make_async_copy(staged, out, left.at[0])
        done.start()
        done.wait()

    if swapped:
        pl.when(place[1] == 0)(run)

        @pl.when(place[1] != 0)
        def _():
            copy = pltpu.make_async_copy(instead, out, left.at[0])
            copy.start()
            copy.wait()

    else:
        run()


def join_product(mine, other, weight, dim, place, instead=()):
    count = weight.shape[1 - dim]
    tiles = count // tile
    half, depth = mine.shape
    return pl.pallas_call(
        functools.partial(join_kernel, dim, bool(instead)),
        in_specs=[scalars] + [anywhere] * (3 + len(instead)),
        out_specs=anywhere,
        out_shape=jax.ShapeDtypeStruct((2 * half, count), bf16),
        scratch_shapes=[
            pltpu.VMEM((2 * half, depth), bf16),
            pltpu.VMEM((2 * half, count), bf16),
            pltpu.SemaphoreType.DMA((tiles + 2,)),
            pltpu.SemaphoreType.DMA((1,)),
            pltpu.VMEM(held_shape(weight, dim), bf16),
        ],
        compiler_params=params,
        cost_estimate=cost,
    )(place, mine, other, weight, *instead)


def lookup_kernel(wanted, table, out, chosen):
    @pl.when(pl.program_id(0) == 0)
    def _():
        row = lax.broadcasted_iota(jnp.int32, chosen.shape, 1)
        chosen[...] = jnp.where(row == wanted[...], 1.0, 0.0).astype(bf16)

    out[...] = multiply(chosen[...], table[...], 0).astype(bf16)


def lookup(wanted, table):
    count = wanted.shape[0]
    rows, feat = table.shape
    return pl.pallas_call(
        lookup_kernel,
        grid=(feat // tile,),
        in_specs=[
            pl.BlockSpec(wanted.shape, lambda i: (0, 0)),
            pl.BlockSpec((rows, tile), lambda i: (0, i)),
        ],
        out_specs=pl.BlockSpec((count, tile), lambda i: (0, i)),
        scratch_shapes=[pltpu.VMEM((count, rows), bf16)],
        out_shape=jax.ShapeDtypeStruct((count, feat), bf16),
        compiler_params=params,
        cost_estimate=cost,
    )(wanted, table)


def tie(*values):
    return lax.optimization_barrier(values)


def after(value, *earlier):
    return lax.optimization_barrier((value, *earlier))[0]


def on_device(token_ids, table, w_up, w_down, cotangent):
    micro, tok, feat = cotangent.shape
    dp = lax.axis_size("dp")
    up = w_up[0]
    down = w_down[0]
    is_first = lax.axis_index("segment") == 0
    here = lax.axis_index("dp")
    place = jnp.stack(
        [lax.axis_index("mp") % 2, lax.axis_index("segment"), here]
    ).astype(jnp.int32)
    capacity = micro * tok
    table_rows = table.shape[0]
    own_cot = cotangent.reshape(capacity, feat)

    def whole(slot):
        return slot.reshape(-1, feat)

    def blocks(rows):
        return rows.reshape(dp, -1, feat)

    def either(left, right):
        return jnp.where(is_first, left, right)

    def chip_sum(kept, sent):
        return (kept.astype(f32) + swap(sent, 1).astype(f32)).astype(bf16)

    def finish(chip, came):
        return chip.astype(f32) + came.astype(f32)

    def active(summed):
        return gelu_value(summed.astype(f32)).astype(bf16)

    def slope(saved, summed):
        return (gelu_slope(saved) * summed.astype(f32)).astype(bf16)

    spot, wanted, most = rank(token_ids.reshape(-1), table_rows, capacity, place)
    fits = most[0, 0] <= capacity

    def sparse():
        return lookup(wanted, table)

    def dense():
        by_owner = token_ids.reshape(micro, dp, tok).transpose(1, 0, 2).reshape(-1, 1)
        fetched = lookup(by_owner - here * table_rows, table)
        return collect(exchange(blocks(fetched))).astype(bf16)

    found = lax.cond(fits, sparse, dense)
    slot_2 = whole(exchange(spread(either(found, own_cot))))
    token = jnp.arange(micro * dp * tok, dtype=jnp.int32)
    in_order = (token // tok % dp) * capacity + token // (dp * tok) * tok + token % tok
    spot = jnp.where(is_first & fits, spot, in_order[:, None])
    spot = spot.reshape(micro, 2, -1).transpose(1, 0, 2).reshape(-1, 1)

    kept, sent, embedded = enter_product(spot, slot_2, up, down, tok, place)
    chip = chip_sum(kept, sent)
    half = chip.shape[0] // 2
    emb_a, emb_b = embedded[:tok], embedded[tok:]
    came_a, came_b = swap(chip[:half], 2), swap(chip[half:], 2)
    first_a = finish(chip[:half], came_a)
    hid_a, first_a = active(first_a), first_a.astype(bf16)
    mix_a = join_product(hid_a, swap(hid_a, 1), down, 0, place)
    slot_4 = exchange(blocks(mix_a))
    first_b = finish(chip[half:], after(came_b, mix_a))
    hid_b, first_b = active(first_b), first_b.astype(bf16)
    act0_a = plus(emb_a, after(slot_4, hid_b))
    pass_a = across(act0_a)
    hid_b = after(hid_b, act0_a)
    mix_b = join_product(hid_b, swap(hid_b, 1), down, 0, place)

    slot_5 = exchange(after(either(blocks(mix_b), spread(pass_a)), slot_4))
    slope_a = gelu_slope(after(first_a, mix_b).astype(f32)).astype(bf16)
    slope_b = gelu_slope(after(first_b, mix_b).astype(f32)).astype(bf16)
    slot_5 = after(slot_5, slope_a, slope_b)
    act0_b = plus(emb_b, slot_5)
    pass_b = across(act0_b)
    kept_a, sent_a = split_product(whole(after(slot_5, act0_b)), up, 0, place)
    pass_b, kept_a, sent_a = tie(pass_b, kept_a, sent_a)
    chip_a = chip_sum(kept_a, sent_a)
    came_a = swap(chip_a, 2)
    slot_6 = exchange(after(spread(after(pass_b, kept_a)), slot_5))
    pre_a = finish(chip_a, came_a)
    back_a = slope(pre_a, first_a)
    pre_a = pre_a.astype(bf16)
    mix_a = join_product(back_a, swap(back_a, 1), up, 1, place)
    kept_b, sent_b = split_product(whole(after(slot_6, mix_a)), up, 0, place)
    slot_7 = exchange(after(blocks(mix_a), slot_6))
    chip_b = chip_sum(kept_b, sent_b)
    came_b = swap(chip_b, 2)
    hid_a = active(after(pre_a, chip_b))
    out_a = join_product(hid_a, swap(hid_a, 1), down, 0, place)
    grad1_a = plus(cotangent[0], after(slot_7, out_a))
    gone_a = across(grad1_a)
    pre_b = finish(chip_b, after(came_b, grad1_a))
    back_b = slope(pre_b, first_b)
    pre_b = pre_b.astype(bf16)
    mix_b = join_product(back_b, swap(back_b, 1), up, 1, place)
    slot_8 = exchange(
        after(either(spread(after(gone_a, mix_b)), blocks(mix_b)), slot_7)
    )
    hid_b = active(after(pre_b, mix_b))
    out_b = join_product(hid_b, swap(hid_b, 1), down, 0, place)
    slot_8 = after(slot_8, out_b)

    grad1_b = plus(cotangent[1], slot_8)
    gone_b = across(grad1_b)
    kept_a, sent_a = split_product(whole(after(slot_8, grad1_b)), down, 1, place)
    send_9 = either(spread(gone_b), blocks(out_a))
    send_9, kept_a, sent_a = tie(send_9, kept_a, sent_a)
    slot_9 = exchange(after(send_9, slot_8))
    chip_a = chip_sum(kept_a, sent_a)
    came_a = swap(chip_a, 2)
    back_a = (slope_a.astype(f32) * finish(chip_a, came_a)).astype(bf16)
    far_a = swap(back_a, 1)
    kept_b, sent_b = split_product(whole(after(slot_9, far_a)), down, 1, place)
    mix_a = join_product(after(back_a, kept_b), far_a, up, 1, place, (out_b,))
    chip_b = chip_sum(after(kept_b, mix_a), sent_b)
    came_b = swap(chip_b, 2)
    slot_10 = exchange(after(blocks(mix_a), slot_9))
    back_b = (slope_b.astype(f32) * finish(chip_b, after(came_b, mix_a))).astype(bf16)
    mix_b = join_product(back_b, swap(back_b, 1), up, 1, place)
    slot_10 = after(slot_10, mix_b)
    slot_11 = exchange(after(blocks(mix_b), slot_10))
    act1_a = plus(pass_a, after(slot_9, mix_b))
    act1_b = plus(pass_b, slot_10)
    grad0_a = plus(gone_a, slot_10)
    grad0_b = plus(gone_b, after(slot_11, act1_a, act1_b, grad0_a))

    acts = jnp.stack([either(act0_a, act1_a), either(act0_b, act1_b)])
    grads = jnp.stack([either(grad0_a, grad1_a), either(grad0_b, grad1_b)])
    return (acts[None], grads[None])


def solution(mesh):
    return jax.shard_map(
        on_device,
        mesh=mesh,
        in_specs=(
            P(),
            P("dp", "mp"),
            P("segment", "mp", "dp"),
            P("segment", "dp", "mp"),
            P(None, "dp", "mp"),
        ),
        out_specs=(P("segment", None, "dp", "mp"), P("segment", None, "dp", "mp")),
        check_vma=False,
    )
```

profile of v0, /device:TPU:0, one launch (start us, length us, event | category | flops | bytes accessed | tf_op | source)
XLA Modules:
  0.0 328.4 jit_solution(17510451161886557044)
XLA Ops:
  3.9 5.1 %conditional.1 = (bf16[32,2048]{1,0:T(8,128)(2,1)S(1)}) conditional(s32[]{:T(128)} %convert_element_type.228, (s32[]{:T(128)}, s32[2,256]{1,0:T(2,128)}, bf16[2048,2048]{1,0:T(8,128)(2,1)}) %tuple.46, (s32[32,1]{1,0:T(8,128)S(1)}, bf16[2048,2048]{1,0:T(8,128)(2,1)}) %tuple.47), branch_computations={%region_0.2_spmd, %region_2.3_spmd} | conditional | flops 200983552 | bytes 7438938 | solution.py:375
  3.9 5.0 %branch_1_fun.1 = bf16[32,2048]{1,0:T(8,128)(2,1)S(1)} custom-call(s32[32,1]{1,0:T(8,128)S(1)} %get-tuple-element.16.wanted, bf16[2048,2048]{1,0:T(8,128)(2,1)} %get-tuple-element.17.table), custom_call_target="tpu_custom_call" | custom-call | flops 200000000 | bytes 1000000 | tf_op jit(solution)/shard_map/cond/branch_1_fun/pallas_call | solution.py:306
  10.6 7.1 %all-to-all-start.1 = ((bf16[16,32,2048]{2,1,0:T(8,128)(2,1)}), bf16[16,32,2048]{2,1,0:T(8,128)(2,1)S(1)}, u32[]{:S(2)}, u32[]{:S(2)}) async-start(bf16[16,32,2048]{2,1,0:T(8,128)(2,1)} %broadcast_in_dim.14), calls=%async_computation.1 | async-start | bytes 4194304 | tf_op jit(solution)/shard_map/all_to_all | solution.py:37
  18.1 30.0 %all-to-all-done.1 = bf16[16,32,2048]{2,1,0:T(8,128)(2,1)S(1)} async-done(((bf16[16,32,2048]{2,1,0:T(8,128)(2,1)}), bf16[16,32,2048]{2,1,0:T(8,128)(2,1)S(1)}, u32[]{:S(2)}, u32[]{:S(2)}) %all-to-all-start.1) | async-done | bytes 2097184 | tf_op jit(solution)/shard_map/all_to_all | solution.py:37
  48.1 8.0 %shard_map.69 = (bf16[256,2048]{1,0:T(8,128)(2,1)S(1)}, bf16[256,2048]{1,0:T(8,128)(2,1)S(1)}, bf16[32,2048]{1,0:T(8,128)(2,1)S(1)}) custom-call(s32[3]{0:T(128)S(1)} %pad_add_fusion.place, s32[512,1]{1,0:T(8,128)S(1)} %copy.13.spot, bf16[512,2048]{1,0:T(8,128)(2,1)S(1)} %bitcast.57, bf16[2048,2048]{1,0:T(8,128)(2,1)} %bitcast.72, bf16[2048,2048]{1,0:T(8,128)(2,1)} %bitcast.65), custom_call_target="tpu_custom_call" | custom-call | flops 200000000 | bytes 1000000 | tf_op jit(solution)/shard_map/pallas_call | solution.py:164
  61.3 12.2 %collective-permute-done.1 = bf16[128,2048]{1,0:T(8,128)(2,1)S(1)} collective-permute-done((bf16[128,2048]{1,0:T(8,128)(2,1)S(1)}, bf16[128,2048]{1,0:T(8,128)(2,1)S(1)}, u32[]{:S(2)}, u32[]{:S(2)}) %collective-permute-start.1) | collective-permute-done | bytes 524320 | tf_op jit(solution)/shard_map/ppermute | solution.py:29
  76.0 6.1 %shard_map.70 = bf16[256,2048]{1,0:T(8,128)(2,1)} custom-call(s32[3]{0:T(128)S(1)} %pad_add_fusion.place, bf16[128,2048]{1,0:T(8,128)(2,1)S(1)} %get-tuple-element.129.mine, bf16[128,2048]{1,0:T(8,128)(2,1)S(1)} %collective-permute-done.2.other, bf16[2048,2048]{1,0:T(8,128)(2,1)} %bitcast.66), custom_call_target="tpu_custom_call" | custom-call | flops 200000000 | bytes 1000000 | tf_op jit(solution)/shard_map/pallas_call | solution.py:277
  82.1 4.4 %all-to-all-start.2 = ((bf16[16,16,2048]{2,1,0:T(8,128)(2,1)}), bf16[16,16,2048]{2,1,0:T(8,128)(2,1)}, u32[]{:S(2)}, u32[]{:S(2)}) async-start(bf16[16,16,2048]{2,1,0:T(8,128)(2,1)} %bitcast.12), calls=%async_computation.2 | async-start | bytes 2097152 | tf_op jit(solution)/shard_map/all_to_all | solution.py:37
  90.1 14.8 %all-to-all-done.2 = bf16[16,16,2048]{2,1,0:T(8,128)(2,1)} async-done(((bf16[16,16,2048]{2,1,0:T(8,128)(2,1)}), bf16[16,16,2048]{2,1,0:T(8,128)(2,1)}, u32[]{:S(2)}, u32[]{:S(2)}) %all-to-all-start.2) | async-done | bytes 1048608 | tf_op jit(solution)/shard_map/all_to_all | solution.py:37
  106.3 3.9 %collective-permute-start.4 = (bf16[16,2048]{1,0:T(8,128)(2,1)S(1)}, bf16[16,2048]{1,0:T(8,128)(2,1)S(1)}, u32[]{:S(2)}, u32[]{:S(2)}) collective-permute-start(bf16[16,2048]{1,0:T(8,128)(2,1)S(1)} %add_convert_fusion.10), channel_id=1, source_target_pairs={{0,64},{64,0},{1,65},{65,1},{2,66},{66,2},{3,67},{67,3},{4,68},{68... | collective-permute-start | bytes 196616 | tf_op jit(solution)/shard_map/ppermute | solution.py:33
  110.2 5.2 %shard_map.71 = bf16[256,2048]{1,0:T(8,128)(2,1)S(1)} custom-call(s32[3]{0:T(128)S(1)} %pad_add_fusion.place, bf16[128,2048]{1,0:T(8,128)(2,1)S(1)} %get-tuple-element.78.mine, bf16[128,2048]{1,0:T(8,128)(2,1)S(1)} %collective-permute-done.5.other, bf16[2048,2048]{1,0:T(8,128)(2,1)} %bitcast.67), custom_call_target="tpu_custom_call" | custom-call | flops 200000000 | bytes 1000000 | tf_op jit(solution)/shard_map/pallas_call | solution.py:277
  120.3 18.3 %all-to-all-done.3 = bf16[16,16,2048]{2,1,0:T(8,128)(2,1)S(1)} async-done(((bf16[16,16,2048]{2,1,0:T(8,128)(2,1)}), bf16[16,16,2048]{2,1,0:T(8,128)(2,1)S(1)}, u32[]{:S(2)}, u32[]{:S(2)}) %all-to-all-start.3) | async-done | bytes 1048608 | tf_op jit(solution)/shard_map/all_to_all | solution.py:37
  140.7 5.2 %shard_map.72 = (bf16[128,2048]{1,0:T(8,128)(2,1)S(1)}, bf16[128,2048]{1,0:T(8,128)(2,1)S(1)}) custom-call(s32[3]{0:T(128)S(1)} %pad_add_fusion.place, bf16[256,2048]{1,0:T(8,128)(2,1)S(1)} %bitcast.55, bf16[2048,2048]{1,0:T(8,128)(2,1)} %bitcast.73), custom_call_target="tpu_custom_call" | custom-call | flops 200000000 | bytes 1000000 | tf_op jit(solution)/shard_map/pallas_call | solution.py:151
  153.9 8.2 %collective-permute-done.8 = bf16[128,2048]{1,0:T(8,128)(2,1)S(1)} collective-permute-done((bf16[128,2048]{1,0:T(8,128)(2,1)S(1)}, bf16[128,2048]{1,0:T(8,128)(2,1)S(1)}, u32[]{:S(2)}, u32[]{:S(2)}) %collective-permute-start.8) | collective-permute-done | bytes 524320 | tf_op jit(solution)/shard_map/ppermute | solution.py:29
  165.6 6.2 %shard_map.73 = bf16[256,2048]{1,0:T(8,128)(2,1)} custom-call(s32[3]{0:T(128)S(1)} %pad_add_fusion.place, bf16[128,2048]{1,0:T(8,128)(2,1)S(1)} %get-tuple-element.132.mine, bf16[128,2048]{1,0:T(8,128)(2,1)S(1)} %collective-permute-done.9.other, bf16[2048,2048]{1,0:T(8,128)(2,1)} %bitcast.74), custom_call_target="tpu_custom_call" | custom-call | flops 200000000 | bytes 1000000 | tf_op jit(solution)/shard_map/pallas_call | solution.py:277
  172.0 5.2 %shard_map.74 = (bf16[128,2048]{1,0:T(8,128)(2,1)S(1)}, bf16[128,2048]{1,0:T(8,128)(2,1)S(1)}) custom-call(s32[3]{0:T(128)S(1)} %pad_add_fusion.place, bf16[256,2048]{1,0:T(8,128)(2,1)S(1)} %bitcast.58, bf16[2048,2048]{1,0:T(8,128)(2,1)} %bitcast.75), custom_call_target="tpu_custom_call" | custom-call | flops 200000000 | bytes 1000000 | tf_op jit(solution)/shard_map/pallas_call | solution.py:151
  177.3 4.5 %all-to-all-start.5 = ((bf16[16,16,2048]{2,1,0:T(8,128)(2,1)}), bf16[16,16,2048]{2,1,0:T(8,128)(2,1)}, u32[]{:S(2)}, u32[]{:S(2)}) async-start(bf16[16,16,2048]{2,1,0:T(8,128)(2,1)} %bitcast.17), calls=%async_computation.5 | async-start | bytes 2097152 | tf_op jit(solution)/shard_map/all_to_all | solution.py:37
  184.3 5.2 %shard_map.75 = bf16[256,2048]{1,0:T(8,128)(2,1)S(1)} custom-call(s32[3]{0:T(128)S(1)} %pad_add_fusion.place, bf16[128,2048]{1,0:T(8,128)(2,1)S(1)} %fusion.25.mine, bf16[128,2048]{1,0:T(8,128)(2,1)S(1)} %collective-permute-done.11.other, bf16[2048,2048]{1,0:T(8,128)(2,1)} %bitcast.68), custom_call_target="tpu_custom_call" | custom-call | flops 200000000 | bytes 1000000 | tf_op jit(solution)/shard_map/pallas_call | solution.py:277
  189.5 11.0 %all-to-all-done.5 = bf16[16,16,2048]{2,1,0:T(8,128)(2,1)} async-done(((bf16[16,16,2048]{2,1,0:T(8,128)(2,1)}), bf16[16,16,2048]{2,1,0:T(8,128)(2,1)}, u32[]{:S(2)}, u32[]{:S(2)}) %all-to-all-start.5) | async-done | bytes 1048608 | tf_op jit(solution)/shard_map/all_to_all | solution.py:37
  205.2 5.3 %shard_map.76 = bf16[256,2048]{1,0:T(8,128)(2,1)S(1)} custom-call(s32[3]{0:T(128)S(1)} %pad_add_fusion.place, bf16[128,2048]{1,0:T(8,128)(2,1)S(1)} %get-tuple-element.131.mine, bf16[128,2048]{1,0:T(8,128)(2,1)S(1)} %collective-permute-done.14.other, bf16[2048,2048]{1,0:T(8,128)(2,1)} %bitcast.76), custom_call_target="tpu_custom_call" | custom-call | flops 200000000 | bytes 1000000 | tf_op jit(solution)/shard_map/pallas_call | solution.py:277
  217.7 5.2 %shard_map.77.refs_0_ = bf16[256,2048]{1,0:T(8,128)(2,1)S(1)} custom-call(s32[3]{0:T(128)S(1)} %pad_add_fusion.place, bf16[128,2048]{1,0:T(8,128)(2,1)S(1)} %fusion.30.mine, bf16[128,2048]{1,0:T(8,128)(2,1)S(1)} %collective-permute-done.15.other, bf16[2048,2048]{1,0:T(8,128)(2,1)} %bitcast.69), custom_call_target="tpu_custom_call" | custom-call | flops 200000000 | bytes 1000000 | tf_op jit(solution)/shard_map/pallas_call | solution.py:277
  222.8 10.8 %all-to-all-done.6 = bf16[16,16,2048]{2,1,0:T(8,128)(2,1)S(1)} async-done(((bf16[16,16,2048]{2,1,0:T(8,128)(2,1)}), bf16[16,16,2048]{2,1,0:T(8,128)(2,1)S(1)}, u32[]{:S(2)}, u32[]{:S(2)}) %all-to-all-start.6) | async-done | bytes 1048608 | tf_op jit(solution)/shard_map/all_to_all | solution.py:37
  235.7 5.3 %shard_map.78 = (bf16[128,2048]{1,0:T(8,128)(2,1)S(1)}, bf16[128,2048]{1,0:T(8,128)(2,1)S(1)}) custom-call(s32[3]{0:T(128)S(1)} %pad_add_fusion.place, bf16[256,2048]{1,0:T(8,128)(2,1)S(1)} %bitcast.54, bf16[2048,2048]{1,0:T(8,128)(2,1)} %bitcast.70), custom_call_target="tpu_custom_call" | custom-call | flops 200000000 | bytes 1000000 | tf_op jit(solution)/shard_map/pallas_call | solution.py:151
  244.7 3.9 %all-to-all-start.7 = ((bf16[16,16,2048]{2,1,0:T(8,128)(2,1)}), bf16[16,16,2048]{2,1,0:T(8,128)(2,1)S(1)}, u32[]{:S(2)}, u32[]{:S(2)}) async-start(bf16[16,16,2048]{2,1,0:T(8,128)(2,1)} %broadcast_select_fusion), calls=%async_computation.7 | async-start | bytes 2097152 | tf_op jit(solution)/shard_map/all_to_all | solution.py:37
  248.6 9.7 %collective-permute-done.18 = bf16[128,2048]{1,0:T(8,128)(2,1)} collective-permute-done((bf16[128,2048]{1,0:T(8,128)(2,1)S(1)}, bf16[128,2048]{1,0:T(8,128)(2,1)}, u32[]{:S(2)}, u32[]{:S(2)}) %collective-permute-start.18) | collective-permute-done | bytes 524320 | tf_op jit(solution)/shard_map/ppermute | solution.py:29
  260.4 6.2 %all-to-all-done.7 = bf16[16,16,2048]{2,1,0:T(8,128)(2,1)S(1)} async-done(((bf16[16,16,2048]{2,1,0:T(8,128)(2,1)}), bf16[16,16,2048]{2,1,0:T(8,128)(2,1)S(1)}, u32[]{:S(2)}, u32[]{:S(2)}) %all-to-all-start.7) | async-done | bytes 1048608 | tf_op jit(solution)/shard_map/all_to_all | solution.py:37
  266.6 5.3 %shard_map.79 = (bf16[128,2048]{1,0:T(8,128)(2,1)S(1)}, bf16[128,2048]{1,0:T(8,128)(2,1)S(1)}) custom-call(s32[3]{0:T(128)S(1)} %pad_add_fusion.place, bf16[256,2048]{1,0:T(8,128)(2,1)S(1)} %bitcast.53, bf16[2048,2048]{1,0:T(8,128)(2,1)} %bitcast.71), custom_call_target="tpu_custom_call" | custom-call | flops 200000000 | bytes 1000000 | tf_op jit(solution)/shard_map/pallas_call | solution.py:151
  272.0 6.2 %shard_map.80 = bf16[256,2048]{1,0:T(8,128)(2,1)} custom-call(s32[3]{0:T(128)S(1)} %pad_add_fusion.place, bf16[128,2048]{1,0:T(8,128)(2,1)S(1)} %multiply_convert_fusion.1.mine, bf16[128,2048]{1,0:T(8,128)(2,1)S(1)} %collective-permute-done.19.other, bf16[2048,2048]{1,0:T(8,128)(2,1)} %bitcast.77, bf16[256,2048]{1,0:T(8,128)(2,1)S(1)} %shard_map.77.refs_0_), custom_call_target="tpu_custom_call" | custom-call | flops 200000000 | bytes 1000000 | tf_op jit(solution)/shard_map/pallas_call | solution.py:277
  283.8 9.1 %collective-permute-done.21 = bf16[128,2048]{1,0:T(8,128)(2,1)} collective-permute-done((bf16[128,2048]{1,0:T(8,128)(2,1)S(1)}, bf16[128,2048]{1,0:T(8,128)(2,1)}, u32[]{:S(2)}, u32[]{:S(2)}) %collective-permute-start.21) | collective-permute-done | bytes 524320 | tf_op jit(solution)/shard_map/ppermute | solution.py:29
  296.8 6.2 %shard_map.81 = bf16[256,2048]{1,0:T(8,128)(2,1)} custom-call(s32[3]{0:T(128)S(1)} %pad_add_fusion.place, bf16[128,2048]{1,0:T(8,128)(2,1)S(1)} %multiply_convert_fusion.mine, bf16[128,2048]{1,0:T(8,128)(2,1)S(1)} %collective-permute-done.22.other, bf16[2048,2048]{1,0:T(8,128)(2,1)} %bitcast.78), custom_call_target="tpu_custom_call" | custom-call | flops 200000000 | bytes 1000000 | tf_op jit(solution)/shard_map/pallas_call | solution.py:277
  303.0 4.5 %all-to-all-start.9 = ((bf16[16,16,2048]{2,1,0:T(8,128)(2,1)}), bf16[16,16,2048]{2,1,0:T(8,128)(2,1)}, u32[]{:S(2)}, u32[]{:S(2)}) async-start(bf16[16,16,2048]{2,1,0:T(8,128)(2,1)} %bitcast.28), calls=%async_computation.9 | async-start | bytes 2097152 | tf_op jit(solution)/shard_map/all_to_all | solution.py:37
  308.6 17.3 %all-to-all-done.9 = bf16[16,16,2048]{2,1,0:T(8,128)(2,1)} async-done(((bf16[16,16,2048]{2,1,0:T(8,128)(2,1)}), bf16[16,16,2048]{2,1,0:T(8,128)(2,1)}, u32[]{:S(2)}, u32[]{:S(2)}) %all-to-all-start.9) | async-done | bytes 1048608 | tf_op jit(solution)/shard_map/all_to_all | solution.py:37
  (115 shorter events, 70.5 us)
Async XLA Ops:
  10.6 37.5 %all-to-all-start.1 = ((bf16[16,32,2048]{2,1,0:T(8,128)(2,1)}), bf16[16,32,2048]{2,1,0:T(8,128)(2,1)S(1)}, u32[]{:S(2)}, u32[]{:S(2)}) async-start(bf16[16,32,2048]{2,1,0:T(8,128)(2,1)} %broadcast_in_dim.14), calls=%async_computation.1 | async-start | bytes 4194304 | tf_op jit(solution)/shard_map/all_to_all | solution.py:37
  56.1 2.7 collective-permute-start
  59.3 14.2 %collective-permute-start.1 = (bf16[128,2048]{1,0:T(8,128)(2,1)S(1)}, bf16[128,2048]{1,0:T(8,128)(2,1)S(1)}, u32[]{:S(2)}, u32[]{:S(2)}) collective-permute-start(bf16[128,2048]{1,0:T(8,128)(2,1)S(1)} %get-tuple-element.134), channel_id=1, source_target_pairs={{0,2},{1,3},{2,0},{3,1},{4,6},{5,7},{6,4},{7,5},{8,10},{9,11},{10,... | collective-permute-start | bytes 1572872 | tf_op jit(solution)/shard_map/ppermute | solution.py:29
  74.0 2.0 collective-permute-start.2
  74.1 14.4 %collective-permute-start.3 = (bf16[128,2048]{1,0:T(8,128)(2,1)S(1)}, bf16[128,2048]{1,0:T(8,128)(2,1)}, u32[]{:S(2)}, u32[]{:S(2)}) collective-permute-start(bf16[128,2048]{1,0:T(8,128)(2,1)S(1)} %get-tuple-element.135), channel_id=1, source_target_pairs={{0,2},{1,3},{2,0},{3,1},{4,6},{5,7},{6,4},{7,5},{8,10},{9,11},{10,... | collective-permute-start | bytes 1572872 | tf_op jit(solution)/shard_map/ppermute | solution.py:29
  82.1 22.7 %all-to-all-start.2 = ((bf16[16,16,2048]{2,1,0:T(8,128)(2,1)}), bf16[16,16,2048]{2,1,0:T(8,128)(2,1)}, u32[]{:S(2)}, u32[]{:S(2)}) async-start(bf16[16,16,2048]{2,1,0:T(8,128)(2,1)} %bitcast.12), calls=%async_computation.2 | async-start | bytes 2097152 | tf_op jit(solution)/shard_map/all_to_all | solution.py:37
  106.2 4.0 %collective-permute-start.5 = (bf16[128,2048]{1,0:T(8,128)(2,1)S(1)}, bf16[128,2048]{1,0:T(8,128)(2,1)S(1)}, u32[]{:S(2)}, u32[]{:S(2)}) collective-permute-start(bf16[128,2048]{1,0:T(8,128)(2,1)S(1)} %get-tuple-element.78.mine), channel_id=1, source_target_pairs={{0,1},{1,0},{2,3},{3,2},{4,5},{5,4},{6,7},{7,6},{8,9},{9,8},{10,11... | collective-permute-start | bytes 1572872 | tf_op jit(solution)/shard_map/ppermute | solution.py:29
  106.3 9.1 %collective-permute-start.4 = (bf16[16,2048]{1,0:T(8,128)(2,1)S(1)}, bf16[16,2048]{1,0:T(8,128)(2,1)S(1)}, u32[]{:S(2)}, u32[]{:S(2)}) collective-permute-start(bf16[16,2048]{1,0:T(8,128)(2,1)S(1)} %add_convert_fusion.10), channel_id=1, source_target_pairs={{0,64},{64,0},{1,65},{65,1},{2,66},{66,2},{3,67},{67,3},{4,68},{68... | collective-permute-start | bytes 196616 | tf_op jit(solution)/shard_map/ppermute | solution.py:33
  116.5 22.2 %all-to-all-start.3 = ((bf16[16,16,2048]{2,1,0:T(8,128)(2,1)}), bf16[16,16,2048]{2,1,0:T(8,128)(2,1)S(1)}, u32[]{:S(2)}, u32[]{:S(2)}) async-start(bf16[16,16,2048]{2,1,0:T(8,128)(2,1)} %broadcast_select_fusion.2), calls=%async_computation.3 | async-start | bytes 2097152 | tf_op jit(solution)/shard_map/all_to_all | solution.py:37
  138.9 7.1 %collective-permute-start.6 = (bf16[16,2048]{1,0:T(8,128)(2,1)S(1)}, bf16[16,2048]{1,0:T(8,128)(2,1)S(1)}, u32[]{:S(2)}, u32[]{:S(2)}) collective-permute-start(bf16[16,2048]{1,0:T(8,128)(2,1)S(1)} %add_convert_fusion.9), channel_id=1, source_target_pairs={{0,64},{64,0},{1,65},{65,1},{2,66},{66,2},{3,67},{67,3},{4,68},{68... | collective-permute-start | bytes 196616 | tf_op jit(solution)/shard_map/ppermute | solution.py:33
  146.0 2.0 collective-permute-start.7
  148.1 14.0 %collective-permute-start.8 = (bf16[128,2048]{1,0:T(8,128)(2,1)S(1)}, bf16[128,2048]{1,0:T(8,128)(2,1)S(1)}, u32[]{:S(2)}, u32[]{:S(2)}) collective-permute-start(bf16[128,2048]{1,0:T(8,128)(2,1)S(1)} %add_convert_fusion.4), channel_id=1, source_target_pairs={{0,2},{1,3},{2,0},{3,1},{4,6},{5,7},{6,4},{7,5},{8,10},{9,11},{10,... | collective-permute-start | bytes 1572872 | tf_op jit(solution)/shard_map/ppermute | solution.py:29
  150.3 21.7 %all-to-all-start.4 = ((bf16[16,16,2048]{2,1,0:T(8,128)(2,1)}), bf16[16,16,2048]{2,1,0:T(8,128)(2,1)S(1)}, u32[]{:S(2)}, u32[]{:S(2)}) async-start(bf16[16,16,2048]{2,1,0:T(8,128)(2,1)} %broadcast_in_dim.16), calls=%async_computation.4 | async-start | bytes 2097152 | tf_op jit(solution)/shard_map/all_to_all | solution.py:37
  163.7 1.9 collective-permute-start.9
  177.2 4.6 %collective-permute-start.10 = (bf16[128,2048]{1,0:T(8,128)(2,1)S(1)}, bf16[128,2048]{1,0:T(8,128)(2,1)S(1)}, u32[]{:S(2)}, u32[]{:S(2)}) collective-permute-start(bf16[128,2048]{1,0:T(8,128)(2,1)S(1)} %get-tuple-element.94), channel_id=1, source_target_pairs={{0,1},{1,0},{2,3},{3,2},{4,5},{5,4},{6,7},{7,6},{8,9},{9,8},{10,11... | collective-permute-start | bytes 1572872 | tf_op jit(solution)/shard_map/ppermute | solution.py:29
  177.3 23.2 %all-to-all-start.5 = ((bf16[16,16,2048]{2,1,0:T(8,128)(2,1)}), bf16[16,16,2048]{2,1,0:T(8,128)(2,1)}, u32[]{:S(2)}, u32[]{:S(2)}) async-start(bf16[16,16,2048]{2,1,0:T(8,128)(2,1)} %bitcast.17), calls=%async_computation.5 | async-start | bytes 2097152 | tf_op jit(solution)/shard_map/all_to_all | solution.py:37
  182.3 2.0 collective-permute-start.11
  182.7 19.1 %collective-permute-start.13 = (bf16[128,2048]{1,0:T(8,128)(2,1)S(1)}, bf16[128,2048]{1,0:T(8,128)(2,1)S(1)}, u32[]{:S(2)}, u32[]{:S(2)}) collective-permute-start(bf16[128,2048]{1,0:T(8,128)(2,1)S(1)} %add_convert_fusion.3), channel_id=1, source_target_pairs={{0,2},{1,3},{2,0},{3,1},{4,6},{5,7},{6,4},{7,5},{8,10},{9,11},{10,... | collective-permute-start | bytes 1572872 | tf_op jit(solution)/shard_map/ppermute | solution.py:29
  202.7 2.5 collective-permute-start.14
  202.8 7.8 %collective-permute-start.12 = (bf16[16,2048]{1,0:T(8,128)(2,1)S(1)}, bf16[16,2048]{1,0:T(8,128)(2,1)S(1)}, u32[]{:S(2)}, u32[]{:S(2)}) collective-permute-start(bf16[16,2048]{1,0:T(8,128)(2,1)S(1)} %fusion.70), channel_id=1, source_target_pairs={{0,64},{64,0},{1,65},{65,1},{2,66},{66,2},{3,67},{67,3},{4,68},{68... | collective-permute-start | bytes 196616 | tf_op jit(solution)/shard_map/ppermute | solution.py:33
  211.6 22.0 %all-to-all-start.6 = ((bf16[16,16,2048]{2,1,0:T(8,128)(2,1)}), bf16[16,16,2048]{2,1,0:T(8,128)(2,1)S(1)}, u32[]{:S(2)}, u32[]{:S(2)}) async-start(bf16[16,16,2048]{2,1,0:T(8,128)(2,1)} %broadcast_select_fusion.1), calls=%async_computation.6 | async-start | bytes 2097152 | tf_op jit(solution)/shard_map/all_to_all | solution.py:37
  215.7 2.0 collective-permute-start.15
  233.8 7.2 %collective-permute-start.16 = (bf16[16,2048]{1,0:T(8,128)(2,1)S(1)}, bf16[16,2048]{1,0:T(8,128)(2,1)S(1)}, u32[]{:S(2)}, u32[]{:S(2)}) collective-permute-start(bf16[16,2048]{1,0:T(8,128)(2,1)S(1)} %fusion.71), channel_id=1, source_target_pairs={{0,64},{64,0},{1,65},{65,1},{2,66},{66,2},{3,67},{67,3},{4,68},{68... | collective-permute-start | bytes 196616 | tf_op jit(solution)/shard_map/ppermute | solution.py:33
  242.1 1.9 collective-permute-start.17
  244.2 14.2 %collective-permute-start.18 = (bf16[128,2048]{1,0:T(8,128)(2,1)S(1)}, bf16[128,2048]{1,0:T(8,128)(2,1)}, u32[]{:S(2)}, u32[]{:S(2)}) collective-permute-start(bf16[128,2048]{1,0:T(8,128)(2,1)S(1)} %add_convert_fusion.2), channel_id=1, source_target_pairs={{0,2},{1,3},{2,0},{3,1},{4,6},{5,7},{6,4},{7,5},{8,10},{9,11},{10,... | collective-permute-start | bytes 1572872 | tf_op jit(solution)/shard_map/ppermute | solution.py:29
  244.7 22.0 %all-to-all-start.7 = ((bf16[16,16,2048]{2,1,0:T(8,128)(2,1)}), bf16[16,16,2048]{2,1,0:T(8,128)(2,1)S(1)}, u32[]{:S(2)}, u32[]{:S(2)}) async-start(bf16[16,16,2048]{2,1,0:T(8,128)(2,1)} %broadcast_select_fusion), calls=%async_computation.7 | async-start | bytes 2097152 | tf_op jit(solution)/shard_map/all_to_all | solution.py:37
  260.3 6.3 %collective-permute-start.19 = (bf16[128,2048]{1,0:T(8,128)(2,1)S(1)}, bf16[128,2048]{1,0:T(8,128)(2,1)S(1)}, u32[]{:S(2)}, u32[]{:S(2)}) collective-permute-start(bf16[128,2048]{1,0:T(8,128)(2,1)S(1)} %multiply_convert_fusion.1.mine), channel_id=1, source_target_pairs={{0,1},{1,0},{2,3},{3,2},{4,5},{5,4},{6,7},{7,6},{8,9},{9,8},{10,11... | collective-permute-start | bytes 1572872 | tf_op jit(solution)/shard_map/ppermute | solution.py:29
  271.9 6.4 %collective-permute-start.20 = (bf16[128,2048]{1,0:T(8,128)(2,1)S(1)}, bf16[128,2048]{1,0:T(8,128)(2,1)S(1)}, u32[]{:S(2)}, u32[]{:S(2)}) collective-permute-start(bf16[128,2048]{1,0:T(8,128)(2,1)S(1)} %get-tuple-element.113), channel_id=1, source_target_pairs={{0,1},{1,0},{2,3},{3,2},{4,5},{5,4},{6,7},{7,6},{8,9},{9,8},{10,11... | collective-permute-start | bytes 1572872 | tf_op jit(solution)/shard_map/ppermute | solution.py:29
  278.4 14.5 %collective-permute-start.21 = (bf16[128,2048]{1,0:T(8,128)(2,1)S(1)}, bf16[128,2048]{1,0:T(8,128)(2,1)}, u32[]{:S(2)}, u32[]{:S(2)}) collective-permute-start(bf16[128,2048]{1,0:T(8,128)(2,1)S(1)} %add_convert_fusion.1), channel_id=1, source_target_pairs={{0,2},{1,3},{2,0},{3,1},{4,6},{5,7},{6,4},{7,5},{8,10},{9,11},{10,... | collective-permute-start | bytes 1572872 | tf_op jit(solution)/shard_map/ppermute | solution.py:29
  280.1 22.9 %all-to-all-start.8 = ((bf16[16,16,2048]{2,1,0:T(8,128)(2,1)}), bf16[16,16,2048]{2,1,0:T(8,128)(2,1)S(1)}, u32[]{:S(2)}, u32[]{:S(2)}) async-start(bf16[16,16,2048]{2,1,0:T(8,128)(2,1)} %bitcast.24), calls=%async_computation.8 | async-start | bytes 2097152 | tf_op jit(solution)/shard_map/all_to_all | solution.py:37
  294.8 2.0 collective-permute-start.22
  303.0 22.9 %all-to-all-start.9 = ((bf16[16,16,2048]{2,1,0:T(8,128)(2,1)}), bf16[16,16,2048]{2,1,0:T(8,128)(2,1)}, u32[]{:S(2)}, u32[]{:S(2)}) async-start(bf16[16,16,2048]{2,1,0:T(8,128)(2,1)} %bitcast.28), calls=%async_computation.9 | async-start | bytes 2097152 | tf_op jit(solution)/shard_map/all_to_all | solution.py:37
  (13 other events, 297.4 us)
where the time goes:
time: 335 us; the launch traced here: 328 us
  waiting for transfers between devices  162 us (48%)
  Pallas kernels  81.2 us (24%)
  starting transfers between devices  59 us (18%)
  other arithmetic  19.6 us (6%)
  local copies, waits for them, and re-layouts  3.87 us (1%)
    all_to_all x9, waiting for transfers between devices, exchange(): return lax.all_to_all(blocks, 'dp', 0, 0)  108 us
    ppermute x19, waiting for transfers between devices, swap(): return lax.ppermute(value, 'mp', [(i, i ^ bit) for i in range(4)])  53.9 us
    pallas_call x8, Pallas kernels, join_product(): pl.pallas_call(functools.partial(join_kernel, dim, bool(instead)), in_spe...  45.6 us
    all_to_all x9, starting transfers between devices, exchange(): return lax.all_to_all(blocks, 'dp', 0, 0)  39.1 us
    pallas_call x4, Pallas kernels, split_product(): pl.pallas_call(functools.partial(split_kernel, dim), in_specs=[scalars, a...  21 us
    ppermute x4, starting transfers between devices, across(): return lax.ppermute(value, 'segment', [(0, 1), (1, 0)])  10.1 us
    ppermute x19, starting transfers between devices, swap(): return lax.ppermute(value, 'mp', [(i, i ^ bit) for i in range(4)])  9.75 us
    pallas_call x1, Pallas kernels, enter_product(): pl.pallas_call(enter_kernel, in_specs=[scalars, in_vmem, anywhere, anywhe...  7.97 us
  transfers between devices with their start and end apart: 32, of which 21 were waited for; matrix products, arithmetic and copies ran while one was open for 4% of the time, Pallas kernels for 17%

commit v1 on v0

--- a/solution.py
+++ b/solution.py
@@ -390,10 +390,9 @@
     slot_4 = exchange(blocks(mix_a))
     first_b = finish(chip[half:], after(came_b, mix_a))
     hid_b, first_b = active(first_b), first_b.astype(bf16)
-    act0_a = plus(emb_a, after(slot_4, hid_b))
+    mix_b = join_product(hid_b, swap(hid_b, 1), down, 0, place)
+    act0_a = plus(emb_a, after(slot_4, mix_b))
     pass_a = across(act0_a)
-    hid_b = after(hid_b, act0_a)
-    mix_b = join_product(hid_b, swap(hid_b, 1), down, 0, place)
 
     slot_5 = exchange(after(either(blocks(mix_b), spread(pass_a)), slot_4))
     slope_a = gelu_slope(after(first_a, mix_b).astype(f32)).astype(bf16)
@@ -437,21 +436,20 @@
     slot_9 = exchange(after(send_9, slot_8))
     chip_a = chip_sum(kept_a, sent_a)
     came_a = swap(chip_a, 2)
-    back_a = (slope_a.astype(f32) * finish(chip_a, came_a)).astype(bf16)
+    kept_b, sent_b = split_product(whole(slot_9), down, 1, place)
+    back_a = (slope_a.astype(f32) * finish(chip_a, after(came_a, kept_b))).astype(bf16)
     far_a = swap(back_a, 1)
-    kept_b, sent_b = split_product(whole(after(slot_9, far_a)), down, 1, place)
-    mix_a = join_product(after(back_a, kept_b), far_a, up, 1, place, (out_b,))
-    chip_b = chip_sum(after(kept_b, mix_a), sent_b)
+    chip_b = chip_sum(kept_b, sent_b)
     came_b = swap(chip_b, 2)
+    mix_a = join_product(after(back_a, chip_b), far_a, up, 1, place, (out_b,))
     slot_10 = exchange(after(blocks(mix_a), slot_9))
-    back_b = (slope_b.astype(f32) * finish(chip_b, after(came_b, mix_a))).astype(bf16)
+    act1_a = plus(pass_a, after(slot_9, mix_a))
+    back_b = (slope_b.astype(f32) * finish(chip_b, after(came_b, act1_a))).astype(bf16)
     mix_b = join_product(back_b, swap(back_b, 1), up, 1, place)
-    slot_10 = after(slot_10, mix_b)
     slot_11 = exchange(after(blocks(mix_b), slot_10))
-    act1_a = plus(pass_a, after(slot_9, mix_b))
     act1_b = plus(pass_b, slot_10)
     grad0_a = plus(gone_a, slot_10)
-    grad0_b = plus(gone_b, after(slot_11, act1_a, act1_b, grad0_a))
+    grad0_b = plus(gone_b, after(slot_11, act1_b, grad0_a))
 
     acts = jnp.stack([either(act0_a, act1_a), either(act0_b, act1_b)])
     grads = jnp.stack([either(grad0_a, grad1_a), either(grad0_b, grad1_b)])

time: 335 us -> 325 us (0.970)
  waiting for transfers between devices: 162 us -> 151 us
    ppermute x19, waiting for transfers between devices: 53.9 us -> 38.9 us  [swap(): return lax.ppermute(value, 'mp', [(i, i ^ bit) for i in range(4)])]
  transfers between devices with their start and end apart: 32 -> 32, of which waited for: 21 -> 23; matrix products, arithmetic and copies ran while one was open for 4% -> 5% of each run, Pallas kernels for 17% -> 19%
where the time goes in v1:
time: 325 us; the launch traced here: 319 us
  waiting for transfers between devices  151 us (46%)
  Pallas kernels  82 us (25%)
  starting transfers between devices  58.3 us (18%)
  other arithmetic  21.1 us (6%)
  local copies, waits for them, and re-layouts  3.87 us (1%)
    all_to_all x9, waiting for transfers between devices, exchange(): return lax.all_to_all(blocks, 'dp', 0, 0)  110 us
    pallas_call x8, Pallas kernels, join_product(): pl.pallas_call(functools.partial(join_kernel, dim, bool(instead)), in_spe...  45.7 us
    ppermute x19, waiting for transfers between devices, swap(): return lax.ppermute(value, 'mp', [(i, i ^ bit) for i in range(4)])  38.9 us
    all_to_all x9, starting transfers between devices, exchange(): return lax.all_to_all(blocks, 'dp', 0, 0)  37.5 us
    pallas_call x4, Pallas kernels, split_product(): pl.pallas_call(functools.partial(split_kernel, dim), in_specs=[scalars, a...  21.7 us
    ppermute x19, starting transfers between devices, swap(): return lax.ppermute(value, 'mp', [(i, i ^ bit) for i in range(4)])  10.6 us
    ppermute x4, starting transfers between devices, across(): return lax.ppermute(value, 'segment', [(0, 1), (1, 0)])  10.1 us
    pallas_call x1, Pallas kernels, enter_product(): pl.pallas_call(enter_kernel, in_specs=[scalars, in_vmem, anywhere, anywhe...  7.97 us
  transfers between devices with their start and end apart: 32, of which 23 were waited for; matrix products, arithmetic and copies ran while one was open for 5% of the time, Pallas kernels for 19%

profile of v1, /device:TPU:0, one launch (start us, length us, event | category | flops | bytes accessed | tf_op | source)
XLA Modules:
  0.0 319.1 jit_solution(17301621631889661944)
XLA Ops:
  3.9 5.1 %conditional.1 = (bf16[32,2048]{1,0:T(8,128)(2,1)S(1)}) conditional(s32[]{:T(128)} %convert_element_type.228, (s32[]{:T(128)}, s32[2,256]{1,0:T(2,128)}, bf16[2048,2048]{1,0:T(8,128)(2,1)}) %tuple.43, (s32[32,1]{1,0:T(8,128)S(1)}, bf16[2048,2048]{1,0:T(8,128)(2,1)}) %tuple.44), branch_computations={%region_0.2_spmd, %region_2.3_spmd} | conditional | flops 200983552 | bytes 7438938 | solution.py:375
  3.9 5.0 %branch_1_fun.1 = bf16[32,2048]{1,0:T(8,128)(2,1)S(1)} custom-call(s32[32,1]{1,0:T(8,128)S(1)} %get-tuple-element.16.wanted, bf16[2048,2048]{1,0:T(8,128)(2,1)} %get-tuple-element.17.table), custom_call_target="tpu_custom_call" | custom-call | flops 200000000 | bytes 1000000 | tf_op jit(solution)/shard_map/cond/branch_1_fun/pallas_call | solution.py:306
  10.6 7.1 %all-to-all-start.1 = ((bf16[16,32,2048]{2,1,0:T(8,128)(2,1)}), bf16[16,32,2048]{2,1,0:T(8,128)(2,1)S(1)}, u32[]{:S(2)}, u32[]{:S(2)}) async-start(bf16[16,32,2048]{2,1,0:T(8,128)(2,1)} %broadcast_in_dim.14), calls=%async_computation.1 | async-start | bytes 4194304 | tf_op jit(solution)/shard_map/all_to_all | solution.py:37
  18.0 30.0 %all-to-all-done.1 = bf16[16,32,2048]{2,1,0:T(8,128)(2,1)S(1)} async-done(((bf16[16,32,2048]{2,1,0:T(8,128)(2,1)}), bf16[16,32,2048]{2,1,0:T(8,128)(2,1)S(1)}, u32[]{:S(2)}, u32[]{:S(2)}) %all-to-all-start.1) | async-done | bytes 2097184 | tf_op jit(solution)/shard_map/all_to_all | solution.py:37
  48.1 8.0 %shard_map.69 = (bf16[256,2048]{1,0:T(8,128)(2,1)S(1)}, bf16[256,2048]{1,0:T(8,128)(2,1)S(1)}, bf16[32,2048]{1,0:T(8,128)(2,1)S(1)}) custom-call(s32[3]{0:T(128)S(1)} %pad_add_fusion.place, s32[512,1]{1,0:T(8,128)S(1)} %copy.13.spot, bf16[512,2048]{1,0:T(8,128)(2,1)S(1)} %bitcast.57, bf16[2048,2048]{1,0:T(8,128)(2,1)} %bitcast.72, bf16[2048,2048]{1,0:T(8,128)(2,1)} %bitcast.65), custom_call_target="tpu_custom_call" | custom-call | flops 200000000 | bytes 1000000 | tf_op jit(solution)/shard_map/pallas_call | solution.py:164
  61.3 12.2 %collective-permute-done.1 = bf16[128,2048]{1,0:T(8,128)(2,1)S(1)} collective-permute-done((bf16[128,2048]{1,0:T(8,128)(2,1)S(1)}, bf16[128,2048]{1,0:T(8,128)(2,1)S(1)}, u32[]{:S(2)}, u32[]{:S(2)}) %collective-permute-start.1) | collective-permute-done | bytes 524320 | tf_op jit(solution)/shard_map/ppermute | solution.py:29
  76.0 6.1 %shard_map.70 = bf16[256,2048]{1,0:T(8,128)(2,1)} custom-call(s32[3]{0:T(128)S(1)} %pad_add_fusion.place, bf16[128,2048]{1,0:T(8,128)(2,1)S(1)} %get-tuple-element.123.mine, bf16[128,2048]{1,0:T(8,128)(2,1)S(1)} %collective-permute-done.2.other, bf16[2048,2048]{1,0:T(8,128)(2,1)} %bitcast.66), custom_call_target="tpu_custom_call" | custom-call | flops 200000000 | bytes 1000000 | tf_op jit(solution)/shard_map/pallas_call | solution.py:277
  82.1 3.7 %all-to-all-start.2 = ((bf16[16,16,2048]{2,1,0:T(8,128)(2,1)}), bf16[16,16,2048]{2,1,0:T(8,128)(2,1)S(1)}, u32[]{:S(2)}, u32[]{:S(2)}) async-start(bf16[16,16,2048]{2,1,0:T(8,128)(2,1)} %bitcast.12), calls=%async_computation.2 | async-start | bytes 2097152 | tf_op jit(solution)/shard_map/all_to_all | solution.py:37
  92.0 5.2 %shard_map.71 = bf16[256,2048]{1,0:T(8,128)(2,1)S(1)} custom-call(s32[3]{0:T(128)S(1)} %pad_add_fusion.place, bf16[128,2048]{1,0:T(8,128)(2,1)S(1)} %get-tuple-element.121.mine, bf16[128,2048]{1,0:T(8,128)(2,1)S(1)} %collective-permute-done.4.other, bf16[2048,2048]{1,0:T(8,128)(2,1)} %bitcast.67), custom_call_target="tpu_custom_call" | custom-call | flops 200000000 | bytes 1000000 | tf_op jit(solution)/shard_map/pallas_call | solution.py:277
  97.2 6.9 %all-to-all-done.2 = bf16[16,16,2048]{2,1,0:T(8,128)(2,1)S(1)} async-done(((bf16[16,16,2048]{2,1,0:T(8,128)(2,1)}), bf16[16,16,2048]{2,1,0:T(8,128)(2,1)S(1)}, u32[]{:S(2)}, u32[]{:S(2)}) %all-to-all-start.2) | async-done | bytes 1048608 | tf_op jit(solution)/shard_map/all_to_all | solution.py:37
  104.2 3.9 %collective-permute-start.5 = (bf16[16,2048]{1,0:T(8,128)(2,1)S(1)}, bf16[16,2048]{1,0:T(8,128)(2,1)S(1)}, u32[]{:S(2)}, u32[]{:S(2)}) collective-permute-start(bf16[16,2048]{1,0:T(8,128)(2,1)S(1)} %add_convert_fusion.10), channel_id=1, source_target_pairs={{0,64},{64,0},{1,65},{65,1},{2,66},{66,2},{3,67},{67,3},{4,68},{68... | collective-permute-start | bytes 196616 | tf_op jit(solution)/shard_map/ppermute | solution.py:33
  111.5 3.8 %all-to-all-start.3 = ((bf16[16,16,2048]{2,1,0:T(8,128)(2,1)}), bf16[16,16,2048]{2,1,0:T(8,128)(2,1)S(1)}, u32[]{:S(2)}, u32[]{:S(2)}) async-start(bf16[16,16,2048]{2,1,0:T(8,128)(2,1)} %broadcast_select_fusion.2), calls=%async_computation.3 | async-start | bytes 2097152 | tf_op jit(solution)/shard_map/all_to_all | solution.py:37
  117.6 12.9 %all-to-all-done.3 = bf16[16,16,2048]{2,1,0:T(8,128)(2,1)S(1)} async-done(((bf16[16,16,2048]{2,1,0:T(8,128)(2,1)}), bf16[16,16,2048]{2,1,0:T(8,128)(2,1)S(1)}, u32[]{:S(2)}, u32[]{:S(2)}) %all-to-all-start.3) | async-done | bytes 1048608 | tf_op jit(solution)/shard_map/all_to_all | solution.py:37
  134.2 5.2 %shard_map.72 = (bf16[128,2048]{1,0:T(8,128)(2,1)S(1)}, bf16[128,2048]{1,0:T(8,128)(2,1)S(1)}) custom-call(s32[3]{0:T(128)S(1)} %pad_add_fusion.place, bf16[256,2048]{1,0:T(8,128)(2,1)S(1)} %bitcast.55, bf16[2048,2048]{1,0:T(8,128)(2,1)} %bitcast.73), custom_call_target="tpu_custom_call" | custom-call | flops 200000000 | bytes 1000000 | tf_op jit(solution)/shard_map/pallas_call | solution.py:151
  147.4 8.3 %collective-permute-done.8 = bf16[128,2048]{1,0:T(8,128)(2,1)} collective-permute-done((bf16[128,2048]{1,0:T(8,128)(2,1)S(1)}, bf16[128,2048]{1,0:T(8,128)(2,1)}, u32[]{:S(2)}, u32[]{:S(2)}) %collective-permute-start.8) | collective-permute-done | bytes 524320 | tf_op jit(solution)/shard_map/ppermute | solution.py:29
  159.6 6.2 %shard_map.73 = bf16[256,2048]{1,0:T(8,128)(2,1)} custom-call(s32[3]{0:T(128)S(1)} %pad_add_fusion.place, bf16[128,2048]{1,0:T(8,128)(2,1)S(1)} %get-tuple-element.126.mine, bf16[128,2048]{1,0:T(8,128)(2,1)S(1)} %collective-permute-done.9.other, bf16[2048,2048]{1,0:T(8,128)(2,1)} %bitcast.74), custom_call_target="tpu_custom_call" | custom-call | flops 200000000 | bytes 1000000 | tf_op jit(solution)/shard_map/pallas_call | solution.py:277
  165.8 5.2 %shard_map.74 = (bf16[128,2048]{1,0:T(8,128)(2,1)S(1)}, bf16[128,2048]{1,0:T(8,128)(2,1)S(1)}) custom-call(s32[3]{0:T(128)S(1)} %pad_add_fusion.place, bf16[256,2048]{1,0:T(8,128)(2,1)S(1)} %bitcast.58, bf16[2048,2048]{1,0:T(8,128)(2,1)} %bitcast.75), custom_call_target="tpu_custom_call" | custom-call | flops 200000000 | bytes 1000000 | tf_op jit(solution)/shard_map/pallas_call | solution.py:151
  171.2 4.3 %all-to-all-start.5 = ((bf16[16,16,2048]{2,1,0:T(8,128)(2,1)}), bf16[16,16,2048]{2,1,0:T(8,128)(2,1)}, u32[]{:S(2)}, u32[]{:S(2)}) async-start(bf16[16,16,2048]{2,1,0:T(8,128)(2,1)} %bitcast.17), calls=%async_computation.5 | async-start | bytes 2097152 | tf_op jit(solution)/shard_map/all_to_all | solution.py:37
  178.1 5.2 %shard_map.75 = bf16[256,2048]{1,0:T(8,128)(2,1)S(1)} custom-call(s32[3]{0:T(128)S(1)} %pad_add_fusion.place, bf16[128,2048]{1,0:T(8,128)(2,1)S(1)} %fusion.25.mine, bf16[128,2048]{1,0:T(8,128)(2,1)S(1)} %collective-permute-done.11.other, bf16[2048,2048]{1,0:T(8,128)(2,1)} %bitcast.68), custom_call_target="tpu_custom_call" | custom-call | flops 200000000 | bytes 1000000 | tf_op jit(solution)/shard_map/pallas_call | solution.py:277
  183.2 11.0 %all-to-all-done.5 = bf16[16,16,2048]{2,1,0:T(8,128)(2,1)} async-done(((bf16[16,16,2048]{2,1,0:T(8,128)(2,1)}), bf16[16,16,2048]{2,1,0:T(8,128)(2,1)}, u32[]{:S(2)}, u32[]{:S(2)}) %all-to-all-start.5) | async-done | bytes 1048608 | tf_op jit(solution)/shard_map/all_to_all | solution.py:37
  199.2 5.3 %shard_map.76 = bf16[256,2048]{1,0:T(8,128)(2,1)S(1)} custom-call(s32[3]{0:T(128)S(1)} %pad_add_fusion.place, bf16[128,2048]{1,0:T(8,128)(2,1)S(1)} %get-tuple-element.125.mine, bf16[128,2048]{1,0:T(8,128)(2,1)S(1)} %collective-permute-done.14.other, bf16[2048,2048]{1,0:T(8,128)(2,1)} %bitcast.76), custom_call_target="tpu_custom_call" | custom-call | flops 200000000 | bytes 1000000 | tf_op jit(solution)/shard_map/pallas_call | solution.py:277
  211.7 5.2 %shard_map.77.refs_0_ = bf16[256,2048]{1,0:T(8,128)(2,1)S(1)} custom-call(s32[3]{0:T(128)S(1)} %pad_add_fusion.place, bf16[128,2048]{1,0:T(8,128)(2,1)S(1)} %fusion.30.mine, bf16[128,2048]{1,0:T(8,128)(2,1)S(1)} %collective-permute-done.15.other, bf16[2048,2048]{1,0:T(8,128)(2,1)} %bitcast.69), custom_call_target="tpu_custom_call" | custom-call | flops 200000000 | bytes 1000000 | tf_op jit(solution)/shard_map/pallas_call | solution.py:277
  216.9 10.8 %all-to-all-done.6 = bf16[16,16,2048]{2,1,0:T(8,128)(2,1)S(1)} async-done(((bf16[16,16,2048]{2,1,0:T(8,128)(2,1)}), bf16[16,16,2048]{2,1,0:T(8,128)(2,1)S(1)}, u32[]{:S(2)}, u32[]{:S(2)}) %all-to-all-start.6) | async-done | bytes 1048608 | tf_op jit(solution)/shard_map/all_to_all | solution.py:37
  229.6 6.0 %shard_map.78 = (bf16[128,2048]{1,0:T(8,128)(2,1)S(1)}, bf16[128,2048]{1,0:T(8,128)(2,1)}) custom-call(s32[3]{0:T(128)S(1)} %pad_add_fusion.place, bf16[256,2048]{1,0:T(8,128)(2,1)S(1)} %bitcast.54, bf16[2048,2048]{1,0:T(8,128)(2,1)} %bitcast.70), custom_call_target="tpu_custom_call" | custom-call | flops 200000000 | bytes 1000000 | tf_op jit(solution)/shard_map/pallas_call | solution.py:151
  236.9 3.8 %all-to-all-start.7 = ((bf16[16,16,2048]{2,1,0:T(8,128)(2,1)}), bf16[16,16,2048]{2,1,0:T(8,128)(2,1)S(1)}, u32[]{:S(2)}, u32[]{:S(2)}) async-start(bf16[16,16,2048]{2,1,0:T(8,128)(2,1)} %broadcast_select_fusion), calls=%async_computation.7 | async-start | bytes 2097152 | tf_op jit(solution)/shard_map/all_to_all | solution.py:37
  243.3 16.0 %all-to-all-done.7 = bf16[16,16,2048]{2,1,0:T(8,128)(2,1)S(1)} async-done(((bf16[16,16,2048]{2,1,0:T(8,128)(2,1)}), bf16[16,16,2048]{2,1,0:T(8,128)(2,1)S(1)}, u32[]{:S(2)}, u32[]{:S(2)}) %all-to-all-start.7) | async-done | bytes 1048608 | tf_op jit(solution)/shard_map/all_to_all | solution.py:37
  259.3 5.3 %shard_map.79 = (bf16[128,2048]{1,0:T(8,128)(2,1)S(1)}, bf16[128,2048]{1,0:T(8,128)(2,1)S(1)}) custom-call(s32[3]{0:T(128)S(1)} %pad_add_fusion.place, bf16[256,2048]{1,0:T(8,128)(2,1)S(1)} %bitcast.53, bf16[2048,2048]{1,0:T(8,128)(2,1)} %bitcast.71), custom_call_target="tpu_custom_call" | custom-call | flops 200000000 | bytes 1000000 | tf_op jit(solution)/shard_map/pallas_call | solution.py:151
  268.1 6.2 %shard_map.80 = bf16[256,2048]{1,0:T(8,128)(2,1)} custom-call(s32[3]{0:T(128)S(1)} %pad_add_fusion.place, bf16[128,2048]{1,0:T(8,128)(2,1)S(1)} %multiply_convert_fusion.1.mine, bf16[128,2048]{1,0:T(8,128)(2,1)S(1)} %collective-permute-done.20.other, bf16[2048,2048]{1,0:T(8,128)(2,1)} %bitcast.77, bf16[256,2048]{1,0:T(8,128)(2,1)S(1)} %shard_map.77.refs_0_), custom_call_target="tpu_custom_call" | custom-call | flops 200000000 | bytes 1000000 | tf_op jit(solution)/shard_map/pallas_call | solution.py:277
  274.6 3.8 %all-to-all-start.8 = ((bf16[16,16,2048]{2,1,0:T(8,128)(2,1)}), bf16[16,16,2048]{2,1,0:T(8,128)(2,1)S(1)}, u32[]{:S(2)}, u32[]{:S(2)}) async-start(bf16[16,16,2048]{2,1,0:T(8,128)(2,1)} %bitcast.24), calls=%async_computation.8 | async-start | bytes 2097152 | tf_op jit(solution)/shard_map/all_to_all | solution.py:37
  284.2 6.2 %shard_map.81 = bf16[256,2048]{1,0:T(8,128)(2,1)} custom-call(s32[3]{0:T(128)S(1)} %pad_add_fusion.place, bf16[128,2048]{1,0:T(8,128)(2,1)S(1)} %multiply_convert_fusion.mine, bf16[128,2048]{1,0:T(8,128)(2,1)S(1)} %collective-permute-done.22.other, bf16[2048,2048]{1,0:T(8,128)(2,1)} %bitcast.78), custom_call_target="tpu_custom_call" | custom-call | flops 200000000 | bytes 1000000 | tf_op jit(solution)/shard_map/pallas_call | solution.py:277
  290.5 6.5 %all-to-all-done.8 = bf16[16,16,2048]{2,1,0:T(8,128)(2,1)S(1)} async-done(((bf16[16,16,2048]{2,1,0:T(8,128)(2,1)}), bf16[16,16,2048]{2,1,0:T(8,128)(2,1)S(1)}, u32[]{:S(2)}, u32[]{:S(2)}) %all-to-all-start.8) | async-done | bytes 1048608 | tf_op jit(solution)/shard_map/all_to_all | solution.py:37
  301.6 16.2 %all-to-all-done.9 = bf16[16,16,2048]{2,1,0:T(8,128)(2,1)S(1)} async-done(((bf16[16,16,2048]{2,1,0:T(8,128)(2,1)}), bf16[16,16,2048]{2,1,0:T(8,128)(2,1)S(1)}, u32[]{:S(2)}, u32[]{:S(2)}) %all-to-all-start.9) | async-done | bytes 1048608 | tf_op jit(solution)/shard_map/all_to_all | solution.py:37
  (125 shorter events, 75.0 us)
Async XLA Ops:
  10.6 37.5 %all-to-all-start.1 = ((bf16[16,32,2048]{2,1,0:T(8,128)(2,1)}), bf16[16,32,2048]{2,1,0:T(8,128)(2,1)S(1)}, u32[]{:S(2)}, u32[]{:S(2)}) async-start(bf16[16,32,2048]{2,1,0:T(8,128)(2,1)} %broadcast_in_dim.14), calls=%async_computation.1 | async-start | bytes 4194304 | tf_op jit(solution)/shard_map/all_to_all | solution.py:37
  56.0 2.7 collective-permute-start
  59.3 14.2 %collective-permute-start.1 = (bf16[128,2048]{1,0:T(8,128)(2,1)S(1)}, bf16[128,2048]{1,0:T(8,128)(2,1)S(1)}, u32[]{:S(2)}, u32[]{:S(2)}) collective-permute-start(bf16[128,2048]{1,0:T(8,128)(2,1)S(1)} %get-tuple-element.128), channel_id=1, source_target_pairs={{0,2},{1,3},{2,0},{3,1},{4,6},{5,7},{6,4},{7,5},{8,10},{9,11},{10,... | collective-permute-start | bytes 1572872 | tf_op jit(solution)/shard_map/ppermute | solution.py:29
  74.0 2.0 collective-permute-start.2
  74.1 14.4 %collective-permute-start.3 = (bf16[128,2048]{1,0:T(8,128)(2,1)S(1)}, bf16[128,2048]{1,0:T(8,128)(2,1)}, u32[]{:S(2)}, u32[]{:S(2)}) collective-permute-start(bf16[128,2048]{1,0:T(8,128)(2,1)S(1)} %get-tuple-element.129), channel_id=1, source_target_pairs={{0,2},{1,3},{2,0},{3,1},{4,6},{5,7},{6,4},{7,5},{8,10},{9,11},{10,... | collective-permute-start | bytes 1572872 | tf_op jit(solution)/shard_map/ppermute | solution.py:29
  82.1 22.0 %all-to-all-start.2 = ((bf16[16,16,2048]{2,1,0:T(8,128)(2,1)}), bf16[16,16,2048]{2,1,0:T(8,128)(2,1)S(1)}, u32[]{:S(2)}, u32[]{:S(2)}) async-start(bf16[16,16,2048]{2,1,0:T(8,128)(2,1)} %bitcast.12), calls=%async_computation.2 | async-start | bytes 2097152 | tf_op jit(solution)/shard_map/all_to_all | solution.py:37
  90.0 2.0 collective-permute-start.4
  104.2 6.2 %collective-permute-start.5 = (bf16[16,2048]{1,0:T(8,128)(2,1)S(1)}, bf16[16,2048]{1,0:T(8,128)(2,1)S(1)}, u32[]{:S(2)}, u32[]{:S(2)}) collective-permute-start(bf16[16,2048]{1,0:T(8,128)(2,1)S(1)} %add_convert_fusion.10), channel_id=1, source_target_pairs={{0,64},{64,0},{1,65},{65,1},{2,66},{66,2},{3,67},{67,3},{4,68},{68... | collective-permute-start | bytes 196616 | tf_op jit(solution)/shard_map/ppermute | solution.py:33
  111.5 19.0 %all-to-all-start.3 = ((bf16[16,16,2048]{2,1,0:T(8,128)(2,1)}), bf16[16,16,2048]{2,1,0:T(8,128)(2,1)S(1)}, u32[]{:S(2)}, u32[]{:S(2)}) async-start(bf16[16,16,2048]{2,1,0:T(8,128)(2,1)} %broadcast_select_fusion.2), calls=%async_computation.3 | async-start | bytes 2097152 | tf_op jit(solution)/shard_map/all_to_all | solution.py:37
  130.7 8.7 %collective-permute-start.6 = (bf16[16,2048]{1,0:T(8,128)(2,1)S(1)}, bf16[16,2048]{1,0:T(8,128)(2,1)S(1)}, u32[]{:S(2)}, u32[]{:S(2)}) collective-permute-start(bf16[16,2048]{1,0:T(8,128)(2,1)S(1)} %add_convert_fusion.9), channel_id=1, source_target_pairs={{0,64},{64,0},{1,65},{65,1},{2,66},{66,2},{3,67},{67,3},{4,68},{68... | collective-permute-start | bytes 196616 | tf_op jit(solution)/shard_map/ppermute | solution.py:33
  139.4 2.0 collective-permute-start.7
  141.5 14.2 %collective-permute-start.8 = (bf16[128,2048]{1,0:T(8,128)(2,1)S(1)}, bf16[128,2048]{1,0:T(8,128)(2,1)}, u32[]{:S(2)}, u32[]{:S(2)}) collective-permute-start(bf16[128,2048]{1,0:T(8,128)(2,1)S(1)} %add_convert_fusion.4), channel_id=1, source_target_pairs={{0,2},{1,3},{2,0},{3,1},{4,6},{5,7},{6,4},{7,5},{8,10},{9,11},{10,... | collective-permute-start | bytes 1572872 | tf_op jit(solution)/shard_map/ppermute | solution.py:29
  143.7 22.1 %all-to-all-start.4 = ((bf16[16,16,2048]{2,1,0:T(8,128)(2,1)}), bf16[16,16,2048]{2,1,0:T(8,128)(2,1)S(1)}, u32[]{:S(2)}, u32[]{:S(2)}) async-start(bf16[16,16,2048]{2,1,0:T(8,128)(2,1)} %broadcast_in_dim.16), calls=%async_computation.4 | async-start | bytes 2097152 | tf_op jit(solution)/shard_map/all_to_all | solution.py:37
  157.6 2.0 collective-permute-start.9
  171.0 4.6 %collective-permute-start.10 = (bf16[128,2048]{1,0:T(8,128)(2,1)S(1)}, bf16[128,2048]{1,0:T(8,128)(2,1)S(1)}, u32[]{:S(2)}, u32[]{:S(2)}) collective-permute-start(bf16[128,2048]{1,0:T(8,128)(2,1)S(1)} %get-tuple-element.90), channel_id=1, source_target_pairs={{0,1},{1,0},{2,3},{3,2},{4,5},{5,4},{6,7},{7,6},{8,9},{9,8},{10,11... | collective-permute-start | bytes 1572872 | tf_op jit(solution)/shard_map/ppermute | solution.py:29
  171.2 23.0 %all-to-all-start.5 = ((bf16[16,16,2048]{2,1,0:T(8,128)(2,1)}), bf16[16,16,2048]{2,1,0:T(8,128)(2,1)}, u32[]{:S(2)}, u32[]{:S(2)}) async-start(bf16[16,16,2048]{2,1,0:T(8,128)(2,1)} %bitcast.17), calls=%async_computation.5 | async-start | bytes 2097152 | tf_op jit(solution)/shard_map/all_to_all | solution.py:37
  176.1 2.0 collective-permute-start.11
  176.5 19.1 %collective-permute-start.13 = (bf16[128,2048]{1,0:T(8,128)(2,1)S(1)}, bf16[128,2048]{1,0:T(8,128)(2,1)S(1)}, u32[]{:S(2)}, u32[]{:S(2)}) collective-permute-start(bf16[128,2048]{1,0:T(8,128)(2,1)S(1)} %add_convert_fusion.3), channel_id=1, source_target_pairs={{0,2},{1,3},{2,0},{3,1},{4,6},{5,7},{6,4},{7,5},{8,10},{9,11},{10,... | collective-permute-start | bytes 1572872 | tf_op jit(solution)/shard_map/ppermute | solution.py:29
  197.3 1.9 collective-permute-start.14
  197.3 7.2 %collective-permute-start.12 = (bf16[16,2048]{1,0:T(8,128)(2,1)S(1)}, bf16[16,2048]{1,0:T(8,128)(2,1)S(1)}, u32[]{:S(2)}, u32[]{:S(2)}) collective-permute-start(bf16[16,2048]{1,0:T(8,128)(2,1)S(1)} %fusion.70), channel_id=1, source_target_pairs={{0,64},{64,0},{1,65},{65,1},{2,66},{66,2},{3,67},{67,3},{4,68},{68... | collective-permute-start | bytes 196616 | tf_op jit(solution)/shard_map/ppermute | solution.py:33
  205.7 22.0 %all-to-all-start.6 = ((bf16[16,16,2048]{2,1,0:T(8,128)(2,1)}), bf16[16,16,2048]{2,1,0:T(8,128)(2,1)S(1)}, u32[]{:S(2)}, u32[]{:S(2)}) async-start(bf16[16,16,2048]{2,1,0:T(8,128)(2,1)} %broadcast_select_fusion.1), calls=%async_computation.6 | async-start | bytes 2097152 | tf_op jit(solution)/shard_map/all_to_all | solution.py:37
  209.7 2.0 collective-permute-start.15
  227.8 7.9 %collective-permute-start.16 = (bf16[16,2048]{1,0:T(8,128)(2,1)S(1)}, bf16[16,2048]{1,0:T(8,128)(2,1)S(1)}, u32[]{:S(2)}, u32[]{:S(2)}) collective-permute-start(bf16[16,2048]{1,0:T(8,128)(2,1)S(1)} %fusion.71), channel_id=1, source_target_pairs={{0,64},{64,0},{1,65},{65,1},{2,66},{66,2},{3,67},{67,3},{4,68},{68... | collective-permute-start | bytes 196616 | tf_op jit(solution)/shard_map/ppermute | solution.py:33
  236.9 3.8 %collective-permute-start.17 = (bf16[128,2048]{1,0:T(8,128)(2,1)}, bf16[128,2048]{1,0:T(8,128)(2,1)}, u32[]{:S(2)}, u32[]{:S(2)}) collective-permute-start(bf16[128,2048]{1,0:T(8,128)(2,1)} %get-tuple-element.104), channel_id=1, source_target_pairs={{0,1},{1,0},{2,3},{3,2},{4,5},{5,4},{6,7},{7,6},{8,9},{9,8},{10,11... | collective-permute-start | bytes 1572872 | tf_op jit(solution)/shard_map/ppermute | solution.py:29
  236.9 22.4 %all-to-all-start.7 = ((bf16[16,16,2048]{2,1,0:T(8,128)(2,1)}), bf16[16,16,2048]{2,1,0:T(8,128)(2,1)S(1)}, u32[]{:S(2)}, u32[]{:S(2)}) async-start(bf16[16,16,2048]{2,1,0:T(8,128)(2,1)} %broadcast_select_fusion), calls=%async_computation.7 | async-start | bytes 2097152 | tf_op jit(solution)/shard_map/all_to_all | solution.py:37
  241.9 22.8 %collective-permute-start.18 = (bf16[128,2048]{1,0:T(8,128)(2,1)S(1)}, bf16[128,2048]{1,0:T(8,128)(2,1)}, u32[]{:S(2)}, u32[]{:S(2)}) collective-permute-start(bf16[128,2048]{1,0:T(8,128)(2,1)S(1)} %add_convert_fusion.2), channel_id=1, source_target_pairs={{0,2},{1,3},{2,0},{3,1},{4,6},{5,7},{6,4},{7,5},{8,10},{9,11},{10,... | collective-permute-start | bytes 1572872 | tf_op jit(solution)/shard_map/ppermute | solution.py:29
  264.6 2.0 collective-permute-start.19
  266.0 2.1 collective-permute-start.20
  266.7 14.2 %collective-permute-start.21 = (bf16[128,2048]{1,0:T(8,128)(2,1)S(1)}, bf16[128,2048]{1,0:T(8,128)(2,1)}, u32[]{:S(2)}, u32[]{:S(2)}) collective-permute-start(bf16[128,2048]{1,0:T(8,128)(2,1)S(1)} %add_convert_fusion.1), channel_id=1, source_target_pairs={{0,2},{1,3},{2,0},{3,1},{4,6},{5,7},{6,4},{7,5},{8,10},{9,11},{10,... | collective-permute-start | bytes 1572872 | tf_op jit(solution)/shard_map/ppermute | solution.py:29
  274.6 22.5 %all-to-all-start.8 = ((bf16[16,16,2048]{2,1,0:T(8,128)(2,1)}), bf16[16,16,2048]{2,1,0:T(8,128)(2,1)S(1)}, u32[]{:S(2)}, u32[]{:S(2)}) async-start(bf16[16,16,2048]{2,1,0:T(8,128)(2,1)} %bitcast.24), calls=%async_computation.8 | async-start | bytes 2097152 | tf_op jit(solution)/shard_map/all_to_all | solution.py:37
  282.2 2.0 collective-permute-start.22
  297.0 20.7 %all-to-all-start.9 = ((bf16[16,16,2048]{2,1,0:T(8,128)(2,1)}), bf16[16,16,2048]{2,1,0:T(8,128)(2,1)S(1)}, u32[]{:S(2)}, u32[]{:S(2)}) async-start(bf16[16,16,2048]{2,1,0:T(8,128)(2,1)} %bitcast.28), calls=%async_computation.9 | async-start | bytes 2097152 | tf_op jit(solution)/shard_map/all_to_all | solution.py:37
  (17 other events, 123.5 us)
